TPU v7x, 32 devices: a whole 2x2x4 slice. The times are simulated.
32 devices in a mesh: grp: 2 (over x), req: 16 (over z, y, core).
Axes of the slice: x: 2, y: 2, z: 4, core: 2. Of those that a mesh axis runs over, the one named last changes fastest.
Arguments:
- xbc: bfloat16 [4096, 9216], P(('grp', 'req')), parts along dimension 0, may hold values from -6 to 6
- dt_raw: float32 [4096, 128], P(('grp', 'req')), parts along dimension 0, may hold values from -6 to 6
- conv_weight: float32 [4, 9216], replicated, may hold values from -3 to 3
- conv_bias: float32 [9216], replicated, may hold values from -3 to 3
- dt_bias: float32 [128], replicated, may hold values from -1 to 1
- a_log: float32 [128], replicated, may hold values from -6 to -2.5
- d_skip: float32 [128], replicated, may hold values from 0.5 to 1.5
- cache_states: bfloat16 [96, 128, 8192], P(('grp', 'req')), parts along dimension 0, may hold values from -24 to 24
- cache_tails: bfloat16 [96, 3, 9216], P(('grp', 'req')), parts along dimension 0, may hold values from -6 to 6
- hit_owner: int32 [32], P('grp'), parts along dimension 0, may hold values from 0 to 15, as said below
- hit_slot: int32 [32], P('grp'), parts along dimension 0, may hold values from 0 to 2, as said below
- hit_spans: int32 [32], P('grp'), parts along dimension 0, may hold values from 0 to 4
- request_of: int32 [32], P(('grp', 'req')), parts along dimension 0, may hold values from 0 to 15, each once
Outputs:
- y_out: bfloat16 [4096, 8192], P(('grp', 'req')), parts along dimension 0
- final_state: bfloat16 [32, 128, 8192], P(('grp', 'req')), parts along dimension 0
There are 2 independent parts, one for each index of `grp`. A program takes and returns all parts, laid end to end along the dimension named above; an argument that names none is the same for every part. Nothing has to cross between parts.
Inputs may be any that keep to these rules, and one draw needn't show every extreme that they name: `hit_owner`: owners are skewed: some devices hold the prefixes of several requests, others of none. `hit_slot`: all requests that name the same owner device name the same slot of it. `request_of`: each request stands on exactly one device.
All inputs are finite; a program needn't handle non-finite values.
Results may differ from a plain program's by a relative error of at most 0.0039.
Values may be sent and summed in bfloat16 or wider, within the bound.
A program may use at most 128 MiB of HBM per device.

v0:
```python
import jax
import jax.numpy as jnp
from jax import lax
from jax.sharding import PartitionSpec as P

HEADS = 128
HEAD_DIM = 64
GROUPS = 4
NST = 128
INNER = 8192


def convolve(xrows, tail, conv_weight, conv_bias):
    rows = xrows.shape[0]
    taps = conv_weight.shape[0]
    extended = jnp.concatenate([tail, xrows], axis=0).astype(jnp.float32)
    conv = jnp.zeros((rows, xrows.shape[1]), jnp.float32) + conv_bias[None, :]
    for k in range(taps):
        conv = conv + conv_weight[k][None, :] * extended[k : k + rows]
    return jax.nn.silu(conv).astype(jnp.bfloat16)


def local_part(conv_out, dt_rows, dt_bias, a_log, d_skip):
    rows = conv_out.shape[0]
    per_group = HEADS // GROUPS
    inputs = conv_out[:, :INNER].reshape(rows, GROUPS, per_group, HEAD_DIM)
    b_part = conv_out[:, INNER : INNER + GROUPS * NST].reshape(rows, GROUPS, NST)
    c_part = conv_out[:, INNER + GROUPS * NST :].reshape(rows, GROUPS, NST)
    step = jax.nn.softplus(dt_rows + dt_bias[None, :])
    cum = jnp.cumsum(step * (-jnp.exp(a_log))[None, :], axis=0)
    scores = jnp.einsum("tgn,sgn->gts", c_part, b_part, preferred_element_type=jnp.float32)
    diff = cum.T[:, :, None] - cum.T[:, None, :]
    causal = lax.broadcasted_iota(jnp.int32, (rows, rows), 0) >= lax.broadcasted_iota(
        jnp.int32, (rows, rows), 1
    )
    decay = jnp.where(causal[None], jnp.exp(jnp.minimum(diff, 0.0)), 0.0)
    mixing = (
        scores[:, None]
        * decay.reshape(GROUPS, per_group, rows, rows)
        * step.T.reshape(GROUPS, per_group, 1, rows)
    ).astype(jnp.bfloat16)
    y_intra = jnp.einsum("gjts,sgjp->tgjp", mixing, inputs, preferred_element_type=jnp.float32)
    y_local = y_intra + d_skip.reshape(1, GROUPS, per_group, 1) * inputs.astype(jnp.float32)
    last = cum[rows - 1]
    carried = (
        (jnp.exp(last[None, :] - cum) * step).reshape(rows, GROUPS, per_group, 1)
        * inputs.astype(jnp.float32)
    ).astype(jnp.bfloat16)
    fresh = jnp.einsum("sgn,sgjp->ngjp", b_part, carried, preferred_element_type=jnp.float32)
    return (y_local, fresh, c_part, cum)


def state_part(start, c_part, cum):
    rows = c_part.shape[0]
    per_group = HEADS // GROUPS
    start_view = start.reshape(NST, GROUPS, per_group, HEAD_DIM)
    y_state = jnp.einsum("tgn,ngjp->tgjp", c_part, start_view, preferred_element_type=jnp.float32)
    y_state = y_state * jnp.exp(cum).reshape(rows, GROUPS, per_group, 1)
    kept = jnp.exp(cum[rows - 1]).reshape(1, GROUPS, per_group, 1) * start_view.astype(jnp.float32)
    return (y_state, kept)


def local(
    xbc,
    dt_raw,
    conv_weight,
    conv_bias,
    dt_bias,
    a_log,
    d_skip,
    cache_states,
    cache_tails,
    hit_owner,
    hit_slot,
    hit_spans,
    request_of,
):
    slots = cache_states.shape[0]
    every_request = lax.all_gather(request_of, "req", axis=0, tiled=True)
    mine = request_of[0]
    own_row = hit_owner[mine] * slots + hit_slot[mine]
    live = hit_spans[mine] > 0
    device = lax.axis_index("req")
    served = jnp.max(jnp.where(hit_owner == device, hit_slot, 0))
    send_states = lax.dynamic_slice_in_dim(cache_states, served, 1, 0)
    wanted_rows = hit_owner[every_request]
    every_tail = lax.all_gather(cache_tails, "req", axis=0, tiled=True)
    tail = lax.dynamic_index_in_dim(every_tail, own_row, 0, keepdims=False)
    state_parts = lax.all_to_all(send_states, "req", split_axis=2, concat_axis=0, tiled=True)
    state_chosen = jnp.take(state_parts, wanted_rows, axis=0)
    start = lax.all_to_all(state_chosen, "req", split_axis=0, concat_axis=2, tiled=True)[0]
    tail = jnp.where(live, tail, jnp.zeros_like(tail))
    start = jnp.where(live, start, jnp.zeros_like(start))
    conv_out = convolve(xbc, tail, conv_weight, conv_bias)
    y_local, fresh, c_part, cum = local_part(conv_out, dt_raw, dt_bias, a_log, d_skip)
    y_state, kept = state_part(start, c_part, cum)
    rows = xbc.shape[0]
    y_out = (y_local + y_state).reshape(rows, INNER).astype(jnp.bfloat16)
    final_state = (kept + fresh).reshape(1, NST, INNER).astype(jnp.bfloat16)
    return (y_out, final_state)


def solution(mesh):
    in_specs = (
        P(("grp", "req"), None),
        P(("grp", "req"), None),
        P(),
        P(),
        P(),
        P(),
        P(),
        P(("grp", "req"), None, None),
        P(("grp", "req"), None, None),
        P("grp"),
        P("grp"),
        P("grp"),
        P(("grp", "req")),
    )
    out_specs = (P(("grp", "req"), None), P(("grp", "req"), None, None))
    return jax.shard_map(local, mesh=mesh, in_specs=in_specs, out_specs=out_specs, check_vma=False)
```

profile of v0, /device:TPU:15, one launch (start us, length us, event | category | flops | bytes accessed | tf_op | source)
XLA Modules:
  0.0 240.6 jit_solution(13793065196203515922)
XLA Ops:
  7.9 1.2 dynamic-slice
  9.1 0.8 dynamic-update-slice
  9.9 7.9 %all-reduce = s32[16]{0:T(128)S(1)} all-reduce(s32[16]{0:T(128)S(1)} %dynamic-update-slice), channel_id=1, replica_groups=mesh['grp'=2,'req'=16] {'req'}, use_global_device_ids=true, to_apply=%add | all-reduce | flops 16 | bytes 128
  17.8 1.3 compare_select_fusion.3
  21.1 1.7 constant_dynamic-slice_fusion
  22.8 6.9 %copy.73 = bf16[1,128,8192]{1,0,2:T(2,128)(2,1)} copy(bf16[1,128,8192]{2,1,0:T(8,128)(2,1)S(1)} %constant_dynamic-slice_fusion) | data formatting | bytes 4194304
  29.7 0.5 broadcast.94
  30.2 45.2 %reduce.4 = bf16[8192,128]{1,0:T(8,128)(2,1)S(1)} reduce(bf16[8192,1,128]{2,1,0:T(2,128)(2,1)} %bitcast.66, bf16[]{:T(256)} %broadcast.94), dimensions={1}, to_apply=%bitcast.55.reduce_sub_computation | reduce | bytes 4194306
  75.4 2.0 reshape.136
  77.4 9.4 %all-to-all-start = ((bf16[16,2,32768]{2,1,0:T(2,128)(2,1)}), bf16[16,2,32768]{2,1,0:T(2,128)(2,1)}, u32[]{:S(2)}, u32[]{:S(2)}) async-start(bf16[16,2,32768]{2,1,0:T(2,128)(2,1)} %reshape.136), calls=%async_computation | async-start | bytes 4194304 | tf_op jit(solution)/shard_map/all_to_all | solution.py:89
  86.9 0.6 dynamic_slice.17
  87.5 0.7 dynamic_slice.18
  89.5 0.7 dynamic_slice.16
  90.1 3.0 %copy.50 = bf16[128,9216]{0,1:T(8,128)(2,1)S(1)} copy(bf16[128,9216]{1,0:T(8,128)(2,1)} %param.13) | data formatting | bytes 4718592 | tf_op args[0]
  93.2 0.7 gather_fusion
  93.9 0.1 broadcast_multiply_fusion
  93.9 0.2 reduce_window_sum.11
  94.1 0.1 exponential_multiply_fusion
  94.2 0.1 copy.60
  94.3 0.1 exp.45
  94.4 0.1 copy.54
  94.5 0.1 copy.53
  94.6 0.1 copy.59
  94.7 0.1 mul.134
  95.5 0.1 fusion.23
  95.7 38.7 %all-to-all-done = bf16[16,2,32768]{2,1,0:T(2,128)(2,1)} async-done(((bf16[16,2,32768]{2,1,0:T(2,128)(2,1)}), bf16[16,2,32768]{2,1,0:T(2,128)(2,1)}, u32[]{:S(2)}, u32[]{:S(2)}) %all-to-all-start) | async-done | bytes 2097184 | tf_op jit(solution)/shard_map/all_to_all | solution.py:89
  134.4 10.4 %reshape.137 = bf16[8192,1,128]{2,1,0:T(2,128)(2,1)} reshape(bf16[16,2,32768]{2,1,0:T(2,128)(2,1)} %all-to-all-done) | data formatting | bytes 4194304
  144.8 3.8 %copy.72 = bf16[1,128,8192]{1,2,0:T(8,128)(2,1)} copy(bf16[1,128,8192]{1,0,2:T(2,128)(2,1)} %bitcast.67) | data formatting | bytes 4194304
  148.6 3.9 %copy.56 = bf16[1,128,16,512]{3,1,2,0:T(8,128)(2,1)} copy(bf16[1,128,16,512]{1,3,2,0:T(8,128)(2,1)} %bitcast.68) | data formatting | bytes 4194304 | tf_op jit(solution)/shard_map/all_to_all | solution.py:89
  152.5 3.6 %gather_fusion.1 = bf16[16,128,512]{2,1,0:T(8,128)(2,1)} fusion(bf16[16,128,512]{2,1,0:T(8,128)(2,1)} %bitcast.69, s32[1024]{0:T(1024)S(1)} %pad_clamp_fusion), kind=kCustom, calls=%fused_computation.1 | custom fusion | bytes 4194368 | tf_op jit(solution)/shard_map/jit(_take)/gather | solution.py:90
  156.1 3.2 %broadcast_select_fusion = bf16[16,128,512]{2,1,0:T(8,128)(2,1)} fusion(bf16[16,128,512]{2,1,0:T(8,128)(2,1)} %gather_fusion.1, pred[16]{0:T(512)(128)(4,1)S(1)} %compare_and_fusion), kind=kLoop, calls=%fused_computation.32 | loop fusion | flops 1048576 | bytes 4194320 | tf_op jit(solution)/shard_map/jit(_take)/select_n | solution.py:90
  159.2 4.9 %all-to-all-start.1 = ((bf16[16,128,512]{2,1,0:T(8,128)(2,1)}), bf16[16,128,512]{2,1,0:T(8,128)(2,1)}, u32[]{:S(2)}, u32[]{:S(2)}) async-start(bf16[16,128,512]{2,1,0:T(8,128)(2,1)} %broadcast_select_fusion), calls=%async_computation.1 | async-start | bytes 4194304 | tf_op jit(solution)/shard_map/all_to_all | solution.py:91
  164.2 0.9 constant_dynamic-slice_fusion.1
  165.1 2.0 copy.74
  167.1 1.7 select_bitcast_fusion
  168.8 1.8 maximum_convert_fusion
  170.7 11.8 %multiply_convert_fusion.1 = bf16[128,9216]{0,1:T(8,128)(2,1)S(1)} fusion(f32[131,9216]{0,1:T(8,128)S(1)} %maximum_convert_fusion, f32[9216]{0:T(1024)S(1)} %bitcast.85, f32[9216]{0:T(1024)S(1)} %bitcast.86, f32[9216]{0:T(1024)S(1)} %bitcast.84, f32[9216]{0:T(1024)S(1)} %bitcast.83, f32[9216]{0:T(1024)S(1)} %copy-done.5), kind=kLoop, calls=%fused_computation.14 | loop fusion | flops 15335424 | bytes 21417984 | tf_op jit(solution)/shard_map/convert_element_type | solution.py:20
  182.4 0.1 slice.57
  182.6 0.2 fusion.24
  182.9 1.0 copy-done.1
  183.9 6.0 %fusion.4 = f32[4,32,64,128]{3,2,1,0:T(8,128)} fusion(bf16[128,4,32,64]{0,3,2,1:T(8,128)(2,1)S(1)} %bitcast.70, f32[4,32,128]{2,1,0:T(8,128)S(1)} %bitcast.88, f32[4,32,128]{2,1,0:T(8,128)S(1)} %bitcast.89, f32[4,128,128]{2,1,0:T(8,128)S(1)} %fusion.24, pred[128,128]{1,0:T(8,128)(4,1)S(1)} %iota_compare_fusion), kind=kOutput, calls=%fused_computation.15 | convolution fusion | flops 281018368 | bytes 6701056 | tf_op jit(solution)/shard_map/gjts,sgjp->tgjp/dot_general | solution.py:42
  189.9 21.7 %all-to-all-done.1 = bf16[16,128,512]{2,1,0:T(8,128)(2,1)} async-done(((bf16[16,128,512]{2,1,0:T(8,128)(2,1)}), bf16[16,128,512]{2,1,0:T(8,128)(2,1)}, u32[]{:S(2)}, u32[]{:S(2)}) %all-to-all-start.1) | async-done | bytes 2097184 | tf_op jit(solution)/shard_map/all_to_all | solution.py:91
  211.7 1.7 select_bitcast_fusion.1
  213.4 2.4 copy.57
  215.8 4.7 %fusion.9 = bf16[128,4,32,64]{0,3,2,1:T(8,128)(2,1)} fusion(bf16[128,4,32,64]{0,3,2,1:T(8,128)(2,1)} %bitcast.73, bf16[128,4,128,1]{0,2,3,1:T(8,128)(2,1)S(1)} %bitcast.81, bf16[128,4,32,64]{0,3,2,1:T(8,128)(2,1)} %bitcast.71, f32[128,4,32]{0,2,1:T(8,128)S(1)} %bitcast.87, f32[4,32]{1,0:T(4,128)S(1)} %exp.45), kind=kOutput, calls=%fused_computation.21 | convolution fusion | flops 275775488 | bytes 6488576 | tf_op jit(solution)/shard_map/sgn,sgjp->ngjp/dot_general | solution.py:49
  220.5 4.1 %copy.63 = bf16[1,128,8192]{2,1,0:T(8,128)(2,1)} copy(bf16[1,128,8192]{1,2,0:T(8,128)(2,1)} %bitcast.76) | data formatting | bytes 4194304
  224.5 5.2 %fusion.7 = bf16[128,4,32,64]{0,3,2,1:T(8,128)(2,1)} fusion(bf16[128,4,32,64]{0,3,2,1:T(8,128)(2,1)S(1)} %bitcast.72, f32[4,32,64,128]{3,2,1,0:T(8,128)} %fusion.4, bf16[128,4,32,64]{0,3,2,1:T(8,128)(2,1)} %bitcast.74, bf16[128,4,128,1]{0,2,3,1:T(8,128)(2,1)S(1)} %bitcast.78, f32[128,4,32]{0,2,1:T(8,128)S(1)} %bitcast.82, f32[4,32]{1,0:T(4,128)S(1)} %mul.134), kind=kOutput, calls=%fused_computation.18 | convolution fusion | flops 274726912 | bytes 10682880 | tf_op jit(solution)/shard_map/tgn,ngjp->tgjp/dot_general | solution.py:57
  229.7 4.1 %copy.62 = bf16[128,8192]{1,0:T(8,128)(2,1)} copy(bf16[128,8192]{0,1:T(8,128)(2,1)} %bitcast.75) | data formatting | bytes 4194304
  (33 shorter events, 0.2 us)
Async XLA Ops:
  7.2 157.0 %all-gather.2.cloned.1.call-start = ((), (), s32[]{:S(2)}) async-start(), calls=%async_computation.2 | async-start | bytes 3760128 | tf_op jit(solution)/shard_map/all_gather | solution.py:87
  75.4 11.5 %copy-start = (s32[16]{0:T(128)S(1)}, s32[16]{0:T(128)}, u32[]{:S(2)}) copy-start(s32[16]{0:T(128)} %param.22) | copy-start | bytes 196
  75.4 12.1 %copy-start.8 = (s32[16]{0:T(128)S(1)}, s32[16]{0:T(128)}, u32[]{:S(2)}) copy-start(s32[16]{0:T(128)} %param.23) | copy-start | bytes 196
  75.4 14.1 %copy-start.9 = (s32[16]{0:T(128)S(1)}, s32[16]{0:T(128)}, u32[]{:S(2)}) copy-start(s32[16]{0:T(128)} %param.24) | copy-start | bytes 196
  77.4 16.4 %copy-start.10 = (f32[128]{0:T(128)S(1)}, f32[128]{0:T(128)}, u32[]{:S(2)}) copy-start(f32[128]{0:T(128)} %param.18) | copy-start | bytes 1540
  77.4 16.4 %copy-start.3 = (f32[128,128]{1,0:T(8,128)S(1)}, f32[128,128]{1,0:T(8,128)}, u32[]{:S(2)}) copy-start(f32[128,128]{1,0:T(8,128)} %param.14) | copy-start | bytes 196612
  77.4 16.5 %copy-start.6 = (f32[128]{0:T(128)S(1)}, f32[128]{0:T(128)}, u32[]{:S(2)}) copy-start(f32[128]{0:T(128)} %param.17) | copy-start | bytes 1540
  77.4 57.0 %all-to-all-start = ((bf16[16,2,32768]{2,1,0:T(2,128)(2,1)}), bf16[16,2,32768]{2,1,0:T(2,128)(2,1)}, u32[]{:S(2)}, u32[]{:S(2)}) async-start(bf16[16,2,32768]{2,1,0:T(2,128)(2,1)} %reshape.136), calls=%async_computation | async-start | bytes 4194304 | tf_op jit(solution)/shard_map/all_to_all | solution.py:89
  86.8 7.8 %copy-start.7 = (f32[128]{0:T(128)S(1)}, f32[128]{0:T(128)}, u32[]{:S(2)}) copy-start(f32[128]{0:T(128)} %param.19) | copy-start | bytes 1540
  86.9 8.7 %copy-start.4 = (f32[4,9216]{1,0:T(4,128)S(1)}, f32[4,9216]{1,0:T(4,128)}, u32[]{:S(2)}) copy-start(f32[4,9216]{1,0:T(4,128)} %param.15) | copy-start | bytes 442372
  159.2 52.4 %all-to-all-start.1 = ((bf16[16,128,512]{2,1,0:T(8,128)(2,1)}), bf16[16,128,512]{2,1,0:T(8,128)(2,1)}, u32[]{:S(2)}, u32[]{:S(2)}) async-start(bf16[16,128,512]{2,1,0:T(8,128)(2,1)} %broadcast_select_fusion), calls=%async_computation.1 | async-start | bytes 4194304 | tf_op jit(solution)/shard_map/all_to_all | solution.py:91
  168.8 1.8 copy-start.5
  182.6 1.3 copy-start.1
  215.8 8.7 %copy-start.2 = (bf16[128,8192]{0,1:T(8,128)(2,1)S(1)}, bf16[128,8192]{0,1:T(8,128)(2,1)}, u32[]{:S(2)}) copy-start(bf16[128,8192]{0,1:T(8,128)(2,1)} %copy-done.1) | copy-start | bytes 6291460
Sparse Core Ops, SparseCore 0:
  10.3 48.3 all-gather.1
where the time goes:
time: 242 us; the launch traced here: 241 us
  other arithmetic  67 us (28%)
  waiting for transfers between devices  60.5 us (25%)
  local copies, waits for them, and re-layouts  55.7 us (23%)
  between operations  19 us (8%)
  matrix products  16.1 us (7%)
  starting transfers between devices  14.4 us (6%)
  blocking collectives  7.91 us (3%)
    unnamed x1, other arithmetic  45.2 us
    unnamed x34, local copies, waits for them, and re-layouts  39.9 us
    all_to_all x1, waiting for transfers between devices, local(): lax.all_to_all(send_states, 'req', split_axis=2, concat_axis=0, tiled=True)  38.7 us
    all_to_all x1, waiting for transfers between devices, local(): lax.all_to_all(state_chosen, 'req', split_axis=0, concat_axis=2, tiled=True)  21.7 us
    convert_element_type x1, other arithmetic, convolve(): return jax.nn.silu(conv).astype(jnp.bfloat16)  11.8 us
    all_to_all x1, starting transfers between devices, local(): lax.all_to_all(send_states, 'req', split_axis=2, concat_axis=0, tiled=True)  9.43 us
    unnamed x1, blocking collectives  7.91 us
    dot_general x1, matrix products, local_part(): jnp.einsum('gjts,sgjp->tgjp', mixing, inputs, preferred_element_type=jnp....  5.99 us
  transfers between devices with their start and end apart: 3, of which 2 were waited for; matrix products, arithmetic and copies ran while one was open for 47% of the time, Pallas kernels for 0%

commit v1 on v0

--- a/solution.py
+++ b/solution.py
@@ -8,6 +8,22 @@
 GROUPS = 4
 NST = 128
 INNER = 8192
+
+
+def swapped_with_each(x, axis, split, join):
+    ways, here = (lax.axis_size(axis), lax.axis_index(axis))
+    width = x.shape[split] // ways
+    dims = list(x.shape)
+    dims[split] = width
+    height = dims[join]
+    dims[join] = height * ways
+    full = jnp.zeros(dims, x.dtype)
+    for mask in range(ways):
+        part = lax.dynamic_slice_in_dim(x, (here ^ mask) * width, width, axis=split)
+        if mask:
+            part = lax.ppermute(part, axis, [(d, d ^ mask) for d in range(ways)])
+        full = lax.dynamic_update_slice_in_dim(full, part, (here ^ mask) * height, axis=join)
+    return full
 
 
 def convolve(xrows, tail, conv_weight, conv_bias):
@@ -88,7 +104,7 @@
     tail = lax.dynamic_index_in_dim(every_tail, own_row, 0, keepdims=False)
     state_parts = lax.all_to_all(send_states, "req", split_axis=2, concat_axis=0, tiled=True)
     state_chosen = jnp.take(state_parts, wanted_rows, axis=0)
-    start = lax.all_to_all(state_chosen, "req", split_axis=0, concat_axis=2, tiled=True)[0]
+    start = swapped_with_each(state_chosen, "req", 0, 2)[0]
     tail = jnp.where(live, tail, jnp.zeros_like(tail))
     start = jnp.where(live, start, jnp.zeros_like(start))
     conv_out = convolve(xbc, tail, conv_weight, conv_bias)

time: 242 us -> 305 us (1.26)
  the two profiles are of different devices: /device:TPU:15 before, /device:TPU:25 now
where the time goes in v1:
time: 305 us; the launch traced here: 304 us
  local copies, waits for them, and re-layouts  85.2 us (28%)
  waiting for transfers between devices  81.3 us (27%)
  other arithmetic  65.4 us (21%)
  starting transfers between devices  36.5 us (12%)
  between operations  19.3 us (6%)
  matrix products  9.54 us (3%)
  blocking collectives  6.49 us (2%)
    all_to_all x1, waiting for transfers between devices, local(): lax.all_to_all(send_states, 'req', split_axis=2, concat_axis=0, tiled=True)  58.3 us
    unnamed x1, other arithmetic  45.2 us
    unnamed x80, local copies, waits for them, and re-layouts  34.5 us
    ppermute x15, starting transfers between devices, swapped_with_each(): part = lax.ppermute(part, axis, [(d, d ^ mask) for d in range(ways)])  26.2 us
    ppermute x15, waiting for transfers between devices, swapped_with_each(): part = lax.ppermute(part, axis, [(d, d ^ mask) for d in range(ways)])  22.5 us
    squeeze x17, local copies, waits for them, and re-layouts, local(): start = swapped_with_each(state_chosen, 'req', 0, 2)[0]  17.2 us
    dynamic_update_slice x16, local copies, waits for them, and re-layouts, swapped_with_each(): lax.dynamic_update_slice_in_dim(full, part, (here ^ mask) * height, axis=...  15.2 us
    convert_element_type x1, other arithmetic, convolve(): return jax.nn.silu(conv).astype(jnp.bfloat16)  11.8 us
  transfers between devices with their start and end apart: 17, of which 7 were waited for; matrix products, arithmetic and copies ran while one was open for 21% of the time, Pallas kernels for 0%

profile of v1, /device:TPU:25, one launch (start us, length us, event | category | flops | bytes accessed | tf_op | source)
XLA Modules:
  0.0 303.7 jit_solution(8010649839610023202)
XLA Ops:
  7.8 1.2 dynamic-slice
  9.8 6.5 %all-reduce = s32[16]{0:T(128)S(1)} all-reduce(s32[16]{0:T(128)S(1)} %dynamic-update-slice), channel_id=1, replica_groups=mesh['grp'=2,'req'=16] {'req'}, use_global_device_ids=true, to_apply=%add | all-reduce | flops 16 | bytes 128
  16.3 1.3 compare_select_fusion.3
  19.6 1.7 constant_dynamic-slice_fusion.15
  21.3 6.9 %copy.117 = bf16[1,128,8192]{1,0,2:T(2,128)(2,1)} copy(bf16[1,128,8192]{2,1,0:T(8,128)(2,1)S(1)} %constant_dynamic-slice_fusion.15) | data formatting | bytes 4194304
  28.7 45.2 %reduce.4 = bf16[8192,128]{1,0:T(8,128)(2,1)S(1)} reduce(bf16[8192,1,128]{2,1,0:T(2,128)(2,1)} %bitcast.79, bf16[]{:T(256)} %broadcast.82), dimensions={1}, to_apply=%bitcast.68.reduce_sub_computation | reduce | bytes 4194306
  73.9 2.0 reshape.163
  75.9 10.0 %all-to-all-start = ((bf16[16,2,32768]{2,1,0:T(2,128)(2,1)}), bf16[16,2,32768]{2,1,0:T(2,128)(2,1)S(1)}, u32[]{:S(2)}, u32[]{:S(2)}) async-start(bf16[16,2,32768]{2,1,0:T(2,128)(2,1)} %reshape.163), calls=%async_computation | async-start | bytes 4194304 | tf_op jit(solution)/shard_map/all_to_all | solution.py:105
  88.3 58.3 %all-to-all-done = bf16[16,2,32768]{2,1,0:T(2,128)(2,1)S(1)} async-done(((bf16[16,2,32768]{2,1,0:T(2,128)(2,1)}), bf16[16,2,32768]{2,1,0:T(2,128)(2,1)S(1)}, u32[]{:S(2)}, u32[]{:S(2)}) %all-to-all-start) | async-done | bytes 2097184 | tf_op jit(solution)/shard_map/all_to_all | solution.py:105
  146.5 6.7 %reshape.164 = bf16[8192,1,128]{2,1,0:T(2,128)(2,1)} reshape(bf16[16,2,32768]{2,1,0:T(2,128)(2,1)S(1)} %all-to-all-done) | data formatting | bytes 4194304
  153.2 2.6 copy.116
  155.8 2.6 copy.85
  158.4 2.3 gather_fusion.1
  161.9 7.9 %collective-permute-start.1 = (bf16[1,128,512]{2,1,0:T(8,128)(2,1)S(1)}, bf16[1,128,512]{2,1,0:T(8,128)(2,1)S(1)}, u32[]{:S(2)}, u32[]{:S(2)}) collective-permute-start(bf16[1,128,512]{2,1,0:T(8,128)(2,1)S(1)} %get-tuple-element.25), channel_id=1, source_target_pairs={{0,2},{1,3},{2,0},{3,1},{4,6},{5,7},{6,4},{7,5},{8,10},{9,11},{10,... | collective-permute-start | bytes 393224 | tf_op jit(solution)/shard_map/ppermute | solution.py:24
  170.3 1.7 collective-permute-start.3
  173.1 1.3 collective-permute-start.5
  174.4 1.7 collective-permute-start.6
  176.8 1.2 collective-permute-start.7
  179.1 2.0 collective-permute-start.9
  181.2 6.7 %collective-permute-done.5 = bf16[1,128,512]{2,1,0:T(8,128)(2,1)S(1)} collective-permute-done((bf16[1,128,512]{2,1,0:T(8,128)(2,1)S(1)}, bf16[1,128,512]{2,1,0:T(8,128)(2,1)S(1)}, u32[]{:S(2)}, u32[]{:S(2)}) %collective-permute-start.5) | collective-permute-done | bytes 131104 | tf_op jit(solution)/shard_map/ppermute | solution.py:24
  187.9 3.0 collective-permute-done.6
  190.9 1.3 collective-permute-start.11
  192.2 2.4 collective-permute-start.12
  194.6 8.2 %collective-permute-done.8 = bf16[1,128,512]{2,1,0:T(8,128)(2,1)S(1)} collective-permute-done((bf16[1,128,512]{2,1,0:T(8,128)(2,1)S(1)}, bf16[1,128,512]{2,1,0:T(8,128)(2,1)S(1)}, u32[]{:S(2)}, u32[]{:S(2)}) %collective-permute-start.8) | collective-permute-done | bytes 131104 | tf_op jit(solution)/shard_map/ppermute | solution.py:24
  202.8 3.8 %collective-permute-done.9 = bf16[1,128,512]{2,1,0:T(8,128)(2,1)S(1)} collective-permute-done((bf16[1,128,512]{2,1,0:T(8,128)(2,1)S(1)}, bf16[1,128,512]{2,1,0:T(8,128)(2,1)S(1)}, u32[]{:S(2)}, u32[]{:S(2)}) %collective-permute-start.9) | collective-permute-done | bytes 131104 | tf_op jit(solution)/shard_map/ppermute | solution.py:24
  206.6 4.9 %collective-permute-start.14 = (bf16[1,128,512]{2,1,0:T(8,128)(2,1)}, bf16[1,128,512]{2,1,0:T(8,128)(2,1)}, u32[]{:S(2)}, u32[]{:S(2)}) collective-permute-start(bf16[1,128,512]{2,1,0:T(8,128)(2,1)} %get-tuple-element.12), channel_id=1, source_target_pairs={{0,15},{1,14},{2,13},{3,12},{4,11},{5,10},{6,9},{7,8},{8,7},{9,6},... | collective-permute-start | bytes 393224 | tf_op jit(solution)/shard_map/ppermute | solution.py:24
  212.8 3.0 %copy.79 = bf16[128,9216]{0,1:T(8,128)(2,1)S(1)} copy(bf16[128,9216]{1,0:T(8,128)(2,1)} %param.13) | data formatting | bytes 4718592 | tf_op args[0]
  217.2 1.3 dynamic_slice.64
  220.6 1.3 mul.182
  222.6 1.2 exp.45
  224.6 1.6 squeeze.45
  229.9 1.6 copy.91
  240.9 1.7 copy.101
  242.6 1.6 constant_dynamic-update-slice_fusion.14
  244.2 1.6 constant_dynamic-update-slice_fusion.13
  245.7 1.6 constant_dynamic-update-slice_fusion.12
  247.3 1.6 constant_dynamic-update-slice_fusion.11
  248.9 1.6 constant_dynamic-update-slice_fusion.10
  257.1 3.0 %broadcast_select_fusion.1 = bf16[128,8192]{0,1:T(8,128)(2,1)} fusion(bf16[128,8192]{0,1:T(8,128)(2,1)} %constant_dynamic-update-slice_fusion, pred[]{:T(512)} %bitcast.2), kind=kLoop, calls=%fused_computation.32 | loop fusion | flops 1048576 | bytes 4194305 | tf_op jit(solution)/shard_map/jit(_where)/select_n | solution.py:109
  261.0 2.0 copy.118
  263.0 1.7 select_bitcast_fusion
  264.8 1.8 maximum_convert_fusion
  266.7 11.8 %multiply_convert_fusion.1 = bf16[128,9216]{0,1:T(8,128)(2,1)S(1)} fusion(f32[131,9216]{0,1:T(8,128)S(1)} %maximum_convert_fusion, f32[9216]{0:T(1024)S(1)} %bitcast.98, f32[9216]{0:T(1024)S(1)} %bitcast.99, f32[9216]{0:T(1024)S(1)} %bitcast.97, f32[9216]{0:T(1024)S(1)} %bitcast.96, f32[9216]{0:T(1024)S(1)} %copy-done.28), kind=kLoop, calls=%fused_computation.14 | loop fusion | flops 15335424 | bytes 21417984 | tf_op jit(solution)/shard_map/convert_element_type | solution.py:36
  279.3 3.0 fusion.4
  282.4 2.4 fusion.7
  284.8 4.1 %copy.106 = bf16[128,8192]{1,0:T(8,128)(2,1)} copy(bf16[128,8192]{0,1:T(8,128)(2,1)} %bitcast.88) | data formatting | bytes 4194304
  288.9 3.9 %fusion.9 = bf16[128,4,32,64]{0,3,2,1:T(8,128)(2,1)} fusion(bf16[128,4,32,64]{0,3,2,1:T(8,128)(2,1)S(1)} %bitcast.84, bf16[128,4,128,1]{0,2,3,1:T(8,128)(2,1)S(1)} %bitcast.94, bf16[128,4,32,64]{0,3,2,1:T(8,128)(2,1)} %bitcast.87, f32[128,4,32]{0,2,1:T(8,128)S(1)} %bitcast.110, f32[4,32]{1,0:T(4,128)S(1)} %copy-done.31), kind=kOutput, calls=%fused_computation.21 | convolution fusion | flops 275775488 | bytes 6488576 | tf_op jit(solution)/shard_map/sgn,sgjp->ngjp/dot_general | solution.py:65
  292.8 4.1 %copy.107 = bf16[1,128,8192]{2,1,0:T(8,128)(2,1)} copy(bf16[1,128,8192]{1,2,0:T(8,128)(2,1)} %bitcast.89) | data formatting | bytes 4194304
  (140 shorter events, 33.6 us)
Async XLA Ops:
  75.9 10.8 %copy-start = (s32[16]{0:T(128)S(1)}, s32[16]{0:T(128)}, u32[]{:S(2)}) copy-start(s32[16]{0:T(128)} %param.22) | copy-start | bytes 196
  75.9 11.5 %copy-start.33 = (f32[128]{0:T(128)S(1)}, f32[128]{0:T(128)}, u32[]{:S(2)}) copy-start(f32[128]{0:T(128)} %param.18) | copy-start | bytes 1540
  75.9 11.5 %copy-start.10 = (f32[4,9216]{1,0:T(4,128)S(1)}, f32[4,9216]{1,0:T(4,128)}, u32[]{:S(2)}) copy-start(f32[4,9216]{1,0:T(4,128)} %param.15) | copy-start | bytes 442372
  75.9 70.6 %all-to-all-start = ((bf16[16,2,32768]{2,1,0:T(2,128)(2,1)}), bf16[16,2,32768]{2,1,0:T(2,128)(2,1)S(1)}, u32[]{:S(2)}, u32[]{:S(2)}) async-start(bf16[16,2,32768]{2,1,0:T(2,128)(2,1)} %reshape.163), calls=%async_computation | async-start | bytes 4194304 | tf_op jit(solution)/shard_map/all_to_all | solution.py:105
  85.9 174.2 %all-gather.2.cloned.1.call-start = ((), (), s32[]{:S(2)}) async-start(), calls=%async_computation.1 | async-start | bytes 3760128 | tf_op jit(solution)/shard_map/all_gather | solution.py:103
  161.0 11.4 %copy-start.5 = (f32[128,128]{1,0:T(8,128)S(1)}, f32[128,128]{1,0:T(8,128)}, u32[]{:S(2)}) copy-start(f32[128,128]{1,0:T(8,128)} %param.14) | copy-start | bytes 196612
  161.0 11.3 %copy-start.30 = (f32[128]{0:T(128)S(1)}, f32[128]{0:T(128)}, u32[]{:S(2)}) copy-start(f32[128]{0:T(128)} %param.17) | copy-start | bytes 1540
  161.0 51.1 %copy-start.32 = (s32[16]{0:T(128)S(1)}, s32[16]{0:T(128)}, u32[]{:S(2)}) copy-start(s32[16]{0:T(128)} %param.23) | copy-start | bytes 196
  161.9 11.1 %collective-permute-start = (bf16[1,128,512]{2,1,0:T(8,128)(2,1)S(1)}, bf16[1,128,512]{2,1,0:T(8,128)(2,1)S(1)}, u32[]{:S(2)}, u32[]{:S(2)}) collective-permute-start(bf16[1,128,512]{2,1,0:T(8,128)(2,1)S(1)} %get-tuple-element.26), channel_id=1, source_target_pairs={{0,1},{1,0},{2,3},{3,2},{4,5},{5,4},{6,7},{7,6},{8,9},{9,8},{10,11... | collective-permute-start | bytes 393224 | tf_op jit(solution)/shard_map/ppermute | solution.py:24
  161.9 12.4 %collective-permute-start.1 = (bf16[1,128,512]{2,1,0:T(8,128)(2,1)S(1)}, bf16[1,128,512]{2,1,0:T(8,128)(2,1)S(1)}, u32[]{:S(2)}, u32[]{:S(2)}) collective-permute-start(bf16[1,128,512]{2,1,0:T(8,128)(2,1)S(1)} %get-tuple-element.25), channel_id=1, source_target_pairs={{0,2},{1,3},{2,0},{3,1},{4,6},{5,7},{6,4},{7,5},{8,10},{9,11},{10,... | collective-permute-start | bytes 393224 | tf_op jit(solution)/shard_map/ppermute | solution.py:24
  169.9 6.9 %collective-permute-start.2 = (bf16[1,128,512]{2,1,0:T(8,128)(2,1)S(1)}, bf16[1,128,512]{2,1,0:T(8,128)(2,1)S(1)}, u32[]{:S(2)}, u32[]{:S(2)}) collective-permute-start(bf16[1,128,512]{2,1,0:T(8,128)(2,1)S(1)} %get-tuple-element.24), channel_id=1, source_target_pairs={{0,3},{1,2},{2,1},{3,0},{4,7},{5,6},{6,5},{7,4},{8,11},{9,10},{10,... | collective-permute-start | bytes 393224 | tf_op jit(solution)/shard_map/ppermute | solution.py:24
  170.3 7.6 %collective-permute-start.3 = (bf16[1,128,512]{2,1,0:T(8,128)(2,1)S(1)}, bf16[1,128,512]{2,1,0:T(8,128)(2,1)S(1)}, u32[]{:S(2)}, u32[]{:S(2)}) collective-permute-start(bf16[1,128,512]{2,1,0:T(8,128)(2,1)S(1)} %get-tuple-element.23), channel_id=1, source_target_pairs={{0,4},{1,5},{2,6},{3,7},{4,0},{5,1},{6,2},{7,3},{8,12},{9,13},{10,... | collective-permute-start | bytes 393224 | tf_op jit(solution)/shard_map/ppermute | solution.py:24
  172.0 7.1 %collective-permute-start.4 = (bf16[1,128,512]{2,1,0:T(8,128)(2,1)S(1)}, bf16[1,128,512]{2,1,0:T(8,128)(2,1)S(1)}, u32[]{:S(2)}, u32[]{:S(2)}) collective-permute-start(bf16[1,128,512]{2,1,0:T(8,128)(2,1)S(1)} %get-tuple-element.22), channel_id=1, source_target_pairs={{0,5},{1,4},{2,7},{3,6},{4,1},{5,0},{6,3},{7,2},{8,13},{9,12},{10,... | collective-permute-start | bytes 393224 | tf_op jit(solution)/shard_map/ppermute | solution.py:24
  173.0 39.7 %copy-start.11 = (bf16[1,128,512]{2,1,0:T(8,128)(2,1)}, bf16[1,128,512]{2,1,0:T(8,128)(2,1)S(1)}, u32[]{:S(2)}) copy-start(bf16[1,128,512]{2,1,0:T(8,128)(2,1)S(1)} %collective-permute-done) | copy-start | bytes 393220
  173.1 14.9 %collective-permute-start.5 = (bf16[1,128,512]{2,1,0:T(8,128)(2,1)S(1)}, bf16[1,128,512]{2,1,0:T(8,128)(2,1)S(1)}, u32[]{:S(2)}, u32[]{:S(2)}) collective-permute-start(bf16[1,128,512]{2,1,0:T(8,128)(2,1)S(1)} %get-tuple-element.21), channel_id=1, source_target_pairs={{0,6},{1,7},{2,4},{3,5},{4,2},{5,3},{6,0},{7,1},{8,14},{9,15},{10,... | collective-permute-start | bytes 393224 | tf_op jit(solution)/shard_map/ppermute | solution.py:24
  174.4 38.4 %copy-start.13 = (bf16[1,128,512]{2,1,0:T(8,128)(2,1)}, bf16[1,128,512]{2,1,0:T(8,128)(2,1)S(1)}, u32[]{:S(2)}) copy-start(bf16[1,128,512]{2,1,0:T(8,128)(2,1)S(1)} %collective-permute-done.1) | copy-start | bytes 393220
  174.4 16.5 %collective-permute-start.6 = (bf16[1,128,512]{2,1,0:T(8,128)(2,1)S(1)}, bf16[1,128,512]{2,1,0:T(8,128)(2,1)S(1)}, u32[]{:S(2)}, u32[]{:S(2)}) collective-permute-start(bf16[1,128,512]{2,1,0:T(8,128)(2,1)S(1)} %get-tuple-element.20), channel_id=1, source_target_pairs={{0,7},{1,6},{2,5},{3,4},{4,3},{5,2},{6,1},{7,0},{8,15},{9,14},{10,... | collective-permute-start | bytes 393224 | tf_op jit(solution)/shard_map/ppermute | solution.py:24
  176.8 36.0 %copy-start.15 = (bf16[1,128,512]{2,1,0:T(8,128)(2,1)}, bf16[1,128,512]{2,1,0:T(8,128)(2,1)S(1)}, u32[]{:S(2)}) copy-start(bf16[1,128,512]{2,1,0:T(8,128)(2,1)S(1)} %collective-permute-done.2) | copy-start | bytes 393220
  176.8 15.4 %collective-permute-start.7 = (bf16[1,128,512]{2,1,0:T(8,128)(2,1)S(1)}, bf16[1,128,512]{2,1,0:T(8,128)(2,1)S(1)}, u32[]{:S(2)}, u32[]{:S(2)}) collective-permute-start(bf16[1,128,512]{2,1,0:T(8,128)(2,1)S(1)} %get-tuple-element.19), channel_id=1, source_target_pairs={{0,8},{1,9},{2,10},{3,11},{4,12},{5,13},{6,14},{7,15},{8,0},{9,1},... | collective-permute-start | bytes 393224 | tf_op jit(solution)/shard_map/ppermute | solution.py:24
  177.9 34.8 %copy-start.17 = (bf16[1,128,512]{2,1,0:T(8,128)(2,1)}, bf16[1,128,512]{2,1,0:T(8,128)(2,1)S(1)}, u32[]{:S(2)}) copy-start(bf16[1,128,512]{2,1,0:T(8,128)(2,1)S(1)} %collective-permute-done.3) | copy-start | bytes 393220
  178.0 24.8 %collective-permute-start.8 = (bf16[1,128,512]{2,1,0:T(8,128)(2,1)S(1)}, bf16[1,128,512]{2,1,0:T(8,128)(2,1)S(1)}, u32[]{:S(2)}, u32[]{:S(2)}) collective-permute-start(bf16[1,128,512]{2,1,0:T(8,128)(2,1)S(1)} %get-tuple-element.18), channel_id=1, source_target_pairs={{0,9},{1,8},{2,11},{3,10},{4,13},{5,12},{6,15},{7,14},{8,1},{9,0},... | collective-permute-start | bytes 393224 | tf_op jit(solution)/shard_map/ppermute | solution.py:24
  179.1 33.6 %copy-start.19 = (bf16[1,128,512]{2,1,0:T(8,128)(2,1)}, bf16[1,128,512]{2,1,0:T(8,128)(2,1)S(1)}, u32[]{:S(2)}) copy-start(bf16[1,128,512]{2,1,0:T(8,128)(2,1)S(1)} %collective-permute-done.4) | copy-start | bytes 393220
  179.1 27.5 %collective-permute-start.9 = (bf16[1,128,512]{2,1,0:T(8,128)(2,1)S(1)}, bf16[1,128,512]{2,1,0:T(8,128)(2,1)S(1)}, u32[]{:S(2)}, u32[]{:S(2)}) collective-permute-start(bf16[1,128,512]{2,1,0:T(8,128)(2,1)S(1)} %get-tuple-element.17), channel_id=1, source_target_pairs={{0,10},{1,11},{2,8},{3,9},{4,14},{5,15},{6,12},{7,13},{8,2},{9,3},... | collective-permute-start | bytes 393224 | tf_op jit(solution)/shard_map/ppermute | solution.py:24
  187.9 24.8 %copy-start.20 = (bf16[1,128,512]{2,1,0:T(8,128)(2,1)}, bf16[1,128,512]{2,1,0:T(8,128)(2,1)S(1)}, u32[]{:S(2)}) copy-start(bf16[1,128,512]{2,1,0:T(8,128)(2,1)S(1)} %collective-permute-done.5) | copy-start | bytes 393220
  187.9 48.8 %collective-permute-start.10 = (bf16[1,128,512]{2,1,0:T(8,128)(2,1)}, bf16[1,128,512]{2,1,0:T(8,128)(2,1)}, u32[]{:S(2)}, u32[]{:S(2)}) collective-permute-start(bf16[1,128,512]{2,1,0:T(8,128)(2,1)} %get-tuple-element.16), channel_id=1, source_target_pairs={{0,11},{1,10},{2,9},{3,8},{4,15},{5,14},{6,13},{7,12},{8,3},{9,2},... | collective-permute-start | bytes 393224 | tf_op jit(solution)/shard_map/ppermute | solution.py:24
  190.9 21.8 %copy-start.21 = (bf16[1,128,512]{2,1,0:T(8,128)(2,1)}, bf16[1,128,512]{2,1,0:T(8,128)(2,1)S(1)}, u32[]{:S(2)}) copy-start(bf16[1,128,512]{2,1,0:T(8,128)(2,1)S(1)} %collective-permute-done.6) | copy-start | bytes 393220
  190.9 46.9 %collective-permute-start.11 = (bf16[1,128,512]{2,1,0:T(8,128)(2,1)S(1)}, bf16[1,128,512]{2,1,0:T(8,128)(2,1)}, u32[]{:S(2)}, u32[]{:S(2)}) collective-permute-start(bf16[1,128,512]{2,1,0:T(8,128)(2,1)S(1)} %get-tuple-element.15), channel_id=1, source_target_pairs={{0,12},{1,13},{2,14},{3,15},{4,8},{5,9},{6,10},{7,11},{8,4},{9,5},... | collective-permute-start | bytes 393224 | tf_op jit(solution)/shard_map/ppermute | solution.py:24
  192.2 20.6 %copy-start.22 = (bf16[1,128,512]{2,1,0:T(8,128)(2,1)}, bf16[1,128,512]{2,1,0:T(8,128)(2,1)S(1)}, u32[]{:S(2)}) copy-start(bf16[1,128,512]{2,1,0:T(8,128)(2,1)S(1)} %collective-permute-done.7) | copy-start | bytes 393220
  192.2 46.6 %collective-permute-start.12 = (bf16[1,128,512]{2,1,0:T(8,128)(2,1)S(1)}, bf16[1,128,512]{2,1,0:T(8,128)(2,1)}, u32[]{:S(2)}, u32[]{:S(2)}) collective-permute-start(bf16[1,128,512]{2,1,0:T(8,128)(2,1)S(1)} %get-tuple-element.14), channel_id=1, source_target_pairs={{0,13},{1,12},{2,15},{3,14},{4,9},{5,8},{6,11},{7,10},{8,5},{9,4},... | collective-permute-start | bytes 393224 | tf_op jit(solution)/shard_map/ppermute | solution.py:24
  202.8 10.0 %copy-start.23 = (bf16[1,128,512]{2,1,0:T(8,128)(2,1)}, bf16[1,128,512]{2,1,0:T(8,128)(2,1)S(1)}, u32[]{:S(2)}) copy-start(bf16[1,128,512]{2,1,0:T(8,128)(2,1)S(1)} %collective-permute-done.8) | copy-start | bytes 393220
  202.8 37.1 %collective-permute-start.13 = (bf16[1,128,512]{2,1,0:T(8,128)(2,1)S(1)}, bf16[1,128,512]{2,1,0:T(8,128)(2,1)}, u32[]{:S(2)}, u32[]{:S(2)}) collective-permute-start(bf16[1,128,512]{2,1,0:T(8,128)(2,1)S(1)} %get-tuple-element.13), channel_id=1, source_target_pairs={{0,14},{1,15},{2,12},{3,13},{4,10},{5,11},{6,8},{7,9},{8,6},{9,7},... | collective-permute-start | bytes 393224 | tf_op jit(solution)/shard_map/ppermute | solution.py:24
  206.6 6.2 %copy-start.24 = (bf16[1,128,512]{2,1,0:T(8,128)(2,1)}, bf16[1,128,512]{2,1,0:T(8,128)(2,1)S(1)}, u32[]{:S(2)}) copy-start(bf16[1,128,512]{2,1,0:T(8,128)(2,1)S(1)} %collective-permute-done.9) | copy-start | bytes 393220
  206.6 34.2 %collective-permute-start.14 = (bf16[1,128,512]{2,1,0:T(8,128)(2,1)}, bf16[1,128,512]{2,1,0:T(8,128)(2,1)}, u32[]{:S(2)}, u32[]{:S(2)}) collective-permute-start(bf16[1,128,512]{2,1,0:T(8,128)(2,1)} %get-tuple-element.12), channel_id=1, source_target_pairs={{0,15},{1,14},{2,13},{3,12},{4,11},{5,10},{6,9},{7,8},{8,7},{9,6},... | collective-permute-start | bytes 393224 | tf_op jit(solution)/shard_map/ppermute | solution.py:24
  215.8 11.1 %copy-start.12 = (bf16[1,128,512]{2,1,0:T(8,128)(2,1)S(1)}, bf16[1,128,512]{2,1,0:T(8,128)(2,1)}, u32[]{:S(2)}) copy-start(bf16[1,128,512]{2,1,0:T(8,128)(2,1)} %copy-done.11) | copy-start | bytes 393220
  215.9 11.8 %copy-start.14 = (bf16[1,128,512]{2,1,0:T(8,128)(2,1)S(1)}, bf16[1,128,512]{2,1,0:T(8,128)(2,1)}, u32[]{:S(2)}) copy-start(bf16[1,128,512]{2,1,0:T(8,128)(2,1)} %copy-done.13) | copy-start | bytes 393220
  215.9 12.5 %copy-start.16 = (bf16[1,128,512]{2,1,0:T(8,128)(2,1)S(1)}, bf16[1,128,512]{2,1,0:T(8,128)(2,1)}, u32[]{:S(2)}) copy-start(bf16[1,128,512]{2,1,0:T(8,128)(2,1)} %copy-done.15) | copy-start | bytes 393220
  224.6 4.5 %copy-start.18 = (bf16[1,128,512]{2,1,0:T(8,128)(2,1)S(1)}, bf16[1,128,512]{2,1,0:T(8,128)(2,1)}, u32[]{:S(2)}) copy-start(bf16[1,128,512]{2,1,0:T(8,128)(2,1)} %copy-done.17) | copy-start | bytes 393220
  242.6 13.8 %copy-start.3 = (bf16[128,512]{0,1:T(8,128)(2,1)S(1)}, bf16[128,512]{0,1:T(8,128)(2,1)}, u32[]{:S(2)}) copy-start(bf16[128,512]{0,1:T(8,128)(2,1)} %copy.101) | copy-start | bytes 393220
  264.8 1.9 copy-start.6
  264.8 1.9 copy-start.7
  264.8 1.9 copy-start.8
  264.8 1.9 copy-start.9
  278.6 3.8 %copy-start.2 = (bf16[128,8192]{0,1:T(8,128)(2,1)}, bf16[128,8192]{0,1:T(8,128)(2,1)S(1)}, u32[]{:S(2)}) copy-start(bf16[128,8192]{0,1:T(8,128)(2,1)S(1)} %slice.57) | copy-start | bytes 6291460
  279.3 3.1 %copy-start.1 = (bf16[128,8192]{0,1:T(8,128)(2,1)S(1)}, bf16[128,8192]{0,1:T(8,128)(2,1)}, u32[]{:S(2)}) copy-start(bf16[128,8192]{0,1:T(8,128)(2,1)} %broadcast_select_fusion.1) | copy-start | bytes 6291460
  279.3 3.1 %copy-start.4 = (f32[128,128]{0,1:T(8,128)S(1)}, f32[128,128]{0,1:T(8,128)}, u32[]{:S(2)}) copy-start(f32[128,128]{0,1:T(8,128)} %copy.103) | copy-start | bytes 196612
  279.3 3.1 %copy-start.29 = (f32[4,32]{1,0:T(4,128)S(1)}, f32[4,32]{1,0:T(4,128)}, u32[]{:S(2)}) copy-start(f32[4,32]{1,0:T(4,128)} %mul.182) | copy-start | bytes 1540
  284.8 4.1 %copy-start.25 = (f32[128,128]{0,1:T(8,128)S(1)}, f32[128,128]{0,1:T(8,128)}, u32[]{:S(2)}) copy-start(f32[128,128]{0,1:T(8,128)} %copy.104) | copy-start | bytes 196612
  284.8 4.1 %copy-start.31 = (f32[4,32]{1,0:T(4,128)S(1)}, f32[4,32]{1,0:T(4,128)}, u32[]{:S(2)}) copy-start(f32[4,32]{1,0:T(4,128)} %exp.45) | copy-start | bytes 1540
  (3 other events, 3.6 us)
Sparse Core Ops, SparseCore 0:
  89.0 66.6 all-gather.1
